TPU v7x, 32 devices: a whole 2x2x4 slice. The times are simulated.
32 devices in a mesh: groups: 2 (over y), cls: 4 (over x, core), proj: 4 (over z).
Axes of the slice: x: 2, y: 2, z: 4, core: 2. Of those that a mesh axis runs over, the one named last changes fastest.
Arguments:
- particles: bfloat16 [512, 4096], P(('groups', 'cls', 'proj')), parts along dimension 0, may hold values from -6 to 6
- classes: int32 [512, 1], P(('groups', 'cls', 'proj')), parts along dimension 0, may hold values from 0 to 3; in each aligned block of 16 rows (0 to 15, 16 to 31, ...) at most 12 rows name the same one
- windows: int32 [512, 2], P(('groups', 'cls', 'proj')), parts along dimension 0, may hold values from -3 to 3
- pose_lists: int32 [512, 8], P(('groups', 'cls', 'proj')), parts along dimension 0, may hold values from 0 to 15, all different within a row
- inverse_noise: bfloat16 [512], P(('groups', 'cls', 'proj')), parts along dimension 0, may hold values from 0.19921875 to 2
- projections: bfloat16 [4, 2048, 4096], P('cls', 'proj'), may hold values from -0.09375 to 0.09375
Outputs:
- posterior: float32 [512, 16, 2048], P(('groups', 'cls', 'proj')), parts along dimension 0
- evidence: float32 [512], P(('groups', 'cls', 'proj')), parts along dimension 0
There are 2 independent parts, one for each index of `groups`. A program takes and returns all parts, laid end to end along the dimension named above; an argument that names none is the same for every part. Nothing has to cross between parts.
Inputs may be any that keep to these rules, and one draw needn't show every extreme that they name: `classes`: within the rows of one device (aligned blocks of 16 rows) no class group is named by more than 12 rows, and in every draw some class group is named by exactly 12 rows of some device. `pose_lists`: each row names 8 different pose blocks.
All inputs are finite; a program needn't handle non-finite values.
Results may differ from a plain program's by a relative error of at most 0.0069.
Values may be sent and summed in bfloat16 or wider, within the bound.
No kernel may reach another device: no remote copies, remote signals or barrier semaphores. Data moves between devices by JAX's collectives and lax.ppermute only.
A program may use at most 128 MiB of HBM per device.

v0:
```python
import math

import jax
import jax.numpy as jnp
from jax import lax
from jax.sharding import PartitionSpec as P

IMG = 64
J = 2048
NB = 16
SW = 4
SH = 16


def wave_table(half, side):
    indices = jnp.arange(half, dtype=jnp.int32)
    wave_y = (indices // side).astype(jnp.float32)
    wave_x = (indices % side - side // 2).astype(jnp.float32)
    return (wave_x, wave_y)


def shift_rows(row_block, centre_x, centre_y, side, across):
    half = row_block.shape[1] // 2
    wave_x, wave_y = wave_table(half, side)
    offsets = jnp.arange(across * across, dtype=jnp.int32)
    offset_x = (offsets % across - across // 2).astype(jnp.float32)
    offset_y = (offsets // across - across // 2).astype(jnp.float32)
    moved_x = centre_x[:, None] + offset_x[None, :]
    moved_y = centre_y[:, None] + offset_y[None, :]
    phases = (moved_x[:, :, None] * wave_x + moved_y[:, :, None] * wave_y) * (2.0 * math.pi / side)
    cosine = jnp.cos(phases)
    sine = jnp.sin(phases)
    real_part = row_block[:, None, :half].astype(jnp.float32)
    imag_part = row_block[:, None, half:].astype(jnp.float32)
    new_real = real_part * cosine + imag_part * sine
    new_imag = imag_part * cosine - real_part * sine
    return jnp.concatenate([new_real, new_imag], axis=2).astype(jnp.bfloat16)


def block_mask(chosen, block_count):
    block_labels = jnp.arange(block_count, dtype=jnp.int32)
    return jnp.max((chosen[:, :, None] == block_labels[None, None, :]).astype(jnp.float32), axis=1)


def exp_terms(scores, details):
    allowed = jnp.repeat(details[:, :NB], J // NB, axis=1)
    allowed = jnp.maximum(allowed, 1.0 - details[:, NB + 3][:, None])
    scaled = scores * details[:, NB + 2][:, None, None]
    return jnp.exp(scaled) * allowed[:, None, :]


def per_device(particles, classes, windows, pose_lists, inverse_noise, projections):
    owners = lax.axis_size("cls")
    particle_count = particles.shape[0]
    row_width = particles.shape[1]
    capacity = 3 * particle_count // owners
    slot_count = owners * capacity
    labels = classes[:, 0]
    positions = jnp.arange(particle_count, dtype=jnp.int32)
    same_class = (labels[:, None] == labels[None, :]) & (positions[None, :] < positions[:, None])
    ranking = jnp.sum(same_class.astype(jnp.int32), axis=1)
    target = labels * capacity + ranking
    selector = (jnp.arange(slot_count, dtype=jnp.int32)[:, None] == target[None, :]).astype(
        jnp.bfloat16
    )
    home_mask = block_mask(pose_lists, NB)
    details = jnp.concatenate(
        [
            home_mask,
            windows.astype(jnp.float32),
            inverse_noise.astype(jnp.float32)[:, None],
            jnp.ones((particle_count, 1), jnp.float32),
        ],
        axis=1,
    ).astype(jnp.bfloat16)
    sent_rows = (
        jnp.dot(selector, particles, preferred_element_type=jnp.float32)
        .astype(jnp.bfloat16)
        .reshape(owners, capacity, row_width)
    )
    sent_details = (
        jnp.dot(selector, details, preferred_element_type=jnp.float32)
        .astype(jnp.bfloat16)
        .reshape(owners, capacity, NB + 4)
    )
    routed_rows, routed_details = (
        lax.all_to_all(sent_rows, "cls", split_axis=0, concat_axis=0, tiled=True),
        lax.all_to_all(sent_details, "cls", split_axis=0, concat_axis=0, tiled=True),
    )
    routed_rows = routed_rows.reshape(slot_count, row_width)
    routed_details = routed_details.reshape(slot_count, NB + 4)
    own_panel = projections[0]
    detail_float = routed_details.astype(jnp.float32)
    shifted = shift_rows(
        routed_rows, detail_float[:, NB], detail_float[:, NB + 1], IMG, SW
    ).reshape(slot_count * SH, row_width)
    part = lax.dot_general(
        shifted,
        lax.all_gather(own_panel, "proj", axis=0, tiled=True),
        (((1,), (1,)), ((), ())),
        preferred_element_type=jnp.float32,
    )
    terms = exp_terms(part.reshape(slot_count, SH, J), detail_float)
    mean_term = jnp.sum(terms, axis=(1, 2)) / (SH * J)
    weights = terms / mean_term[:, None, None]
    log_mean = jnp.log(mean_term)
    back_weights, back_logs = (
        lax.all_to_all(
            weights.reshape(owners, capacity, SH, J), "cls", split_axis=0, concat_axis=0, tiled=True
        ),
        lax.all_to_all(
            log_mean.reshape(owners, capacity, 1), "cls", split_axis=0, concat_axis=0, tiled=True
        ),
    )
    flat_weights = back_weights.reshape(slot_count, SH, J)
    flat_logs = back_logs.reshape(slot_count)
    posterior = jnp.take(flat_weights, target, axis=0)
    evidence = jnp.take(flat_logs, target, axis=0)
    return (posterior, evidence)


def solution(mesh):
    placed = (
        P(("groups", "cls", "proj"), None),
        P(("groups", "cls", "proj"), None),
        P(("groups", "cls", "proj"), None),
        P(("groups", "cls", "proj"), None),
        P(("groups", "cls", "proj")),
        P("cls", "proj", None),
    )
    return jax.shard_map(
        per_device,
        mesh=mesh,
        in_specs=placed,
        out_specs=(P(("groups", "cls", "proj"), None, None), P(("groups", "cls", "proj"))),
        check_vma=False,
    )
```

profile of v0, /device:TPU:0, one launch (start us, length us, event | category | flops | bytes accessed | tf_op | source)
XLA Modules:
  0.0 416.3 jit_solution(6817408038691435096)
XLA Ops:
  7.2 0.0 copy-start
  7.2 0.0 all-gather.3.cloned.1.call-start
  7.2 0.7 all-gather.3.cloned.1.call-update
  7.9 0.8 copy.23
  8.7 0.7 convert_convert_fusion
  9.4 0.1 copy.24
  9.5 0.7 copy.25
  10.2 0.1 pad.5.clone
  10.3 0.9 convert_reduce_fusion.1
  11.2 0.1 convert_reduce_fusion
  11.3 0.7 multiply_add_fusion
  12.0 0.3 convolution_convert_fusion.1
  12.2 0.1 reshape.206
  12.3 0.7 copy.26
  13.0 4.2 %all-to-all-start.1 = ((bf16[4,12,20]{2,1,0:T(8,128)(2,1)}), bf16[4,12,20]{2,1,0:T(8,128)(2,1)S(1)}, u32[]{:S(2)}, u32[]{:S(2)}) async-start(bf16[4,12,20]{2,1,0:T(8,128)(2,1)} %copy.26), calls=%async_computation.1 | async-start | bytes 32768 | tf_op jit(solution)/shard_map/all_to_all | solution.py:88
  17.2 0.0 copy-done
  17.3 0.2 convolution_convert_fusion
  17.5 0.9 reshape.204
  18.4 2.7 all-to-all-done.1
  21.1 3.5 all-to-all-start
  24.6 0.1 fusion.34
  24.7 0.1 copy.37
  24.8 0.2 broadcast_in_dim.15
  25.0 0.9 bitcast_maximum_fusion
  25.9 0.1 copy.31
  25.9 0.1 copy.32
  26.0 0.1 copy.33
  26.1 0.1 broadcast_add_fusion
  26.2 7.2 %all-to-all-done = bf16[4,12,4096]{2,1,0:T(8,128)(2,1)S(1)} async-done(((bf16[4,12,4096]{2,1,0:T(8,128)(2,1)}), bf16[4,12,4096]{2,1,0:T(8,128)(2,1)S(1)}, u32[]{:S(2)}, u32[]{:S(2)}) %all-to-all-start) | async-done | bytes 393248 | tf_op jit(solution)/shard_map/all_to_all | solution.py:87
  33.4 0.1 reshape.205
  33.5 0.1 slice_convert_fusion.1
  33.6 26.2 %add_convert_fusion = (bf16[48,16,2048]{2,1,0:T(8,128)(2,1)S(1)}, bf16[48,16,2048]{2,1,0:T(8,128)(2,1)}) fusion(f32[48,2048]{1,0:T(8,128)S(1)} %get-tuple-element.7, f32[2048]{0:T(1024)S(1)} %get-tuple-element.19, f32[48,16]{1,0:T(8,128)S(1)} %get-tuple-element.16, f32[2048]{0:T(1024)S(1)} %get-tuple-element.18, f32[48,16]{1,0:T(8,128)S(1)} %get-tuple-element.17, ...), kind=kLoop, calls=%fused_computation.9 | loop fusion | flops 18874368 | bytes 7100416 | tf_op jit(solution)/shard_map/convert.2
  59.7 239.3 %all-gather.3.cloned.1.call-done = bf16[1,2048,4096]{2,1,0:T(8,128)(2,1)} async-done(((bf16[1,512,4096]{2,1,0:T(8,128)(2,1)}), bf16[1,2048,4096]{2,1,0:T(8,128)(2,1)}) %all-gather.3.cloned.1.call-update) | async-done | bytes 16777232 | tf_op jit(solution)/shard_map/all_gather | solution.py:99
  299.1 20.0 %fusion.8 = (f32[48]{0:T(128)S(1)}, f32[48,16,2048]{2,1,0:T(8,128)}) fusion(f32[48,2048]{1,0:T(8,128)} %bitcast_maximum_fusion, f32[48]{0:T(128)S(1)} %bitcast.38, bf16[1,2048,4096]{2,1,0:T(8,128)(2,1)} %all-gather.3.cloned.1.call-done, bf16[48,16,2048]{2,1,0:T(8,128)(2,1)} %get-tuple-element.5, bf16[48,16,2048]{2,1,0:T(8,128)(2,1)S(1)} %get-tuple-element.4), kind=kOutput, calls=%fused_computation.14 | convolution fusion | flops 12902203392 | bytes 29753728 | tf_op jit(solution)/shard_map/dot_general | solution.py:97
  319.1 0.7 log.14
  319.7 3.2 all-to-all-start.3
  323.0 5.4 %fusion.7 = f32[48,16,2048]{2,1,0:T(8,128)} fusion(f32[48,16,2048]{2,1,0:T(8,128)} %get-tuple-element.15, f32[48]{0:T(128)S(1)} %get-tuple-element.13, f32[48,2048]{1,0:T(8,128)} %bitcast_maximum_fusion, f32[48]{0:T(128)S(1)} %bitcast.39), kind=kLoop, calls=%fused_computation.13 | loop fusion | flops 4718592 | bytes 12976512 | tf_op jit(solution)/shard_map/div | solution.py:105
  328.3 0.0 all-to-all-done.3
  328.4 5.4 %all-to-all-start.2 = ((f32[4,12,16,2048]{3,2,1,0:T(8,128)}), f32[4,12,16,2048]{3,2,1,0:T(8,128)}, u32[]{:S(2)}, u32[]{:S(2)}) async-start(f32[4,12,16,2048]{3,2,1,0:T(8,128)} %bitcast.35), calls=%async_computation.2 | async-start | bytes 12582912 | tf_op jit(solution)/shard_map/all_to_all | solution.py:108
  333.7 0.0 copy-done.1
  333.8 0.5 broadcast.254
  334.3 0.7 reduce.3
  335.0 0.1 reshape.210
  335.0 0.7 gather_fusion.1
  335.7 0.5 broadcast_select_fusion.1
  336.2 68.2 %all-to-all-done.2 = f32[4,12,16,2048]{3,2,1,0:T(8,128)} async-done(((f32[4,12,16,2048]{3,2,1,0:T(8,128)}), f32[4,12,16,2048]{3,2,1,0:T(8,128)}, u32[]{:S(2)}, u32[]{:S(2)}) %all-to-all-start.2) | async-done | bytes 6291488 | tf_op jit(solution)/shard_map/all_to_all | solution.py:108
  404.4 3.5 gather_fusion
  407.9 1.6 broadcast_select_fusion
  (8 shorter events, 0.1 us)
Async XLA Ops:
  7.2 10.1 %copy-start = (bf16[16,4096]{1,0:T(8,128)(2,1)S(1)}, bf16[16,4096]{1,0:T(8,128)(2,1)}, u32[]{:S(2)}) copy-start(bf16[16,4096]{1,0:T(8,128)(2,1)} %param.6) | copy-start | bytes 393220
  7.2 291.9 %all-gather.3.cloned.1.call-start = ((), (), s32[]{:S(2)}) async-start(), calls=%async_computation.4 | async-start | bytes 20971520 | tf_op jit(solution)/shard_map/all_gather | solution.py:99
  13.0 8.1 %all-to-all-start.1 = ((bf16[4,12,20]{2,1,0:T(8,128)(2,1)}), bf16[4,12,20]{2,1,0:T(8,128)(2,1)S(1)}, u32[]{:S(2)}, u32[]{:S(2)}) async-start(bf16[4,12,20]{2,1,0:T(8,128)(2,1)} %copy.26), calls=%async_computation.1 | async-start | bytes 32768 | tf_op jit(solution)/shard_map/all_to_all | solution.py:88
  21.1 12.3 %all-to-all-start = ((bf16[4,12,4096]{2,1,0:T(8,128)(2,1)}), bf16[4,12,4096]{2,1,0:T(8,128)(2,1)S(1)}, u32[]{:S(2)}, u32[]{:S(2)}) async-start(bf16[4,12,4096]{2,1,0:T(8,128)(2,1)} %reshape.204), calls=%async_computation | async-start | bytes 1048576 | tf_op jit(solution)/shard_map/all_to_all | solution.py:87
  319.7 8.6 %all-to-all-start.3 = ((f32[4,12,1]{1,2,0:T(1,128)}), f32[4,12,1]{1,2,0:T(1,128)S(1)}, u32[]{:S(2)}, u32[]{:S(2)}) async-start(f32[4,12,1]{1,2,0:T(1,128)} %bitcast.13), calls=%async_computation.3 | async-start | bytes 4096 | tf_op jit(solution)/shard_map/all_to_all | solution.py:111
  328.4 5.4 %copy-start.1 = (s32[16,1]{0,1:T(1,128)S(1)}, s32[16,1]{0,1:T(1,128)}, u32[]{:S(2)}) copy-start(s32[16,1]{0,1:T(1,128)} %param.7) | copy-start | bytes 196
  328.4 76.1 %all-to-all-start.2 = ((f32[4,12,16,2048]{3,2,1,0:T(8,128)}), f32[4,12,16,2048]{3,2,1,0:T(8,128)}, u32[]{:S(2)}, u32[]{:S(2)}) async-start(f32[4,12,16,2048]{3,2,1,0:T(8,128)} %bitcast.35), calls=%async_computation.2 | async-start | bytes 12582912 | tf_op jit(solution)/shard_map/all_to_all | solution.py:108
Sparse Core Ops, SparseCore 0:
  9.6 289.4 all-gather.2
where the time goes:
time: 417 us; the launch traced here: 416 us
  waiting for transfers between devices  318 us (76%)
  other arithmetic  37.8 us (9%)
  matrix products  20.5 us (5%)
  starting transfers between devices  16.3 us (4%)
  between operations  14.2 us (3%)
  local copies, waits for them, and re-layouts  9.34 us (2%)
    all_gather x1, waiting for transfers between devices, per_device(): lax.all_gather(own_panel, 'proj', axis=0, tiled=True)  239 us
    all_to_all x1, waiting for transfers between devices, per_device(): lax.all_to_all(weights.reshape(owners, capacity, SH, J), 'cls', split_axi...  68.2 us
    another operation x2, other arithmetic  26.8 us
    dot_general x1, matrix products, per_device(): lax.dot_general(shifted, lax.all_gather(own_panel, 'proj', axis=0, tiled=...  20 us
  transfers between devices with their start and end apart: 5, of which 4 were waited for; matrix products, arithmetic and copies ran while one was open for 10% of the time, Pallas kernels for 0%

commit v1 on v0

v1 whole, which is shorter than its diff:
```python
import functools
import math

import jax
import jax.numpy as jnp
import numpy as np
from jax import lax
from jax.experimental import pallas as pl
from jax.experimental.pallas import tpu as pltpu
from jax.sharding import PartitionSpec as P

IMG = 64
KF = 2048
J = 2048
NB = 16
SW = 4
SH = 16
LANES = 128
HALVES = 2 * KF // LANES
TILE = 16
BLOCK = J // NB
CHUNKS = 1
BF16_MAX = float(jnp.finfo(jnp.bfloat16).max)


def relative_tables():
    c = np.arange(KF)
    kx, ky = c % IMG - IMG // 2, c // IMG
    s = np.arange(SH)
    turn = (s % SW - SW // 2)[:, None] * kx + (s // SW - SW // 2)[:, None] * ky
    phase = (turn % IMG) * (2.0 * math.pi / IMG)
    return np.cos(phase).astype(np.float32), np.sin(phase).astype(np.float32)


def score_kernel(
    me_ref, rows_ref, own_hbm, other_hbm, cos_ref, sin_ref, out_ref,
    centred, panels, shifted, scores, details, facts, members, panel_sems, fact_sem,
):
    pieces, count, _ = rows_ref.shape
    load = [
        pltpu.make_async_copy(own_hbm, panels.at[0], panel_sems.at[0]),
        pltpu.make_async_copy(other_hbm, panels.at[1], panel_sems.at[1]),
    ]
    load[0].start()
    load[1].start()
    for s in range(pieces):
        details[s * count:(s + 1) * count, :] = rows_ref[s, :, 2 * KF:].astype(jnp.float32)
    send = pltpu.make_async_copy(details, facts, fact_sem)
    send.start()

    lane = lax.broadcasted_iota(jnp.int32, (count, LANES), 1)
    kx = (lane % IMG - IMG // 2).astype(jnp.float32)
    odd = (lane // IMG).astype(jnp.float32)
    unit = 2.0 * math.pi / IMG
    for s in range(pieces):
        fact = details[s * count:(s + 1) * count, :]
        wx = jnp.broadcast_to(fact[:, 1:2], (count, LANES))
        wy = jnp.broadcast_to(fact[:, 2:3], (count, LANES))
        angle = (wx * kx + wy * odd) * unit
        step = wy * (2.0 * unit)
        cosine, sine = jnp.cos(angle), jnp.sin(angle)
        step_cos, step_sin = jnp.cos(step), jnp.sin(step)
        for t in range(KF // LANES):
            at = slice(t * LANES, (t + 1) * LANES)
            to = slice(KF + t * LANES, KF + (t + 1) * LANES)
            re = rows_ref[s, :, at].astype(jnp.float32)
            im = rows_ref[s, :, to].astype(jnp.float32)
            centred[pl.ds(s * count * HALVES + t, count, HALVES), :] = re * cosine + im * sine
            centred[pl.ds(s * count * HALVES + HALVES // 2 + t, count, HALVES), :] = im * cosine - re * sine
            cosine, sine = (
                cosine * step_cos - sine * step_sin,
                sine * step_cos + cosine * step_sin,
            )
    send.wait()

    own = me_ref[0]
    first_block = me_ref[1]

    def sort_row(row, filled):
        label = facts[row, 0].astype(jnp.int32)
        members[0, filled[0]] = row
        members[1, filled[1]] = row
        return (
            filled[0] + (label == own).astype(jnp.int32),
            filled[1] + (label == own + 1 - 2 * (own % 2)).astype(jnp.int32),
        )

    totals = lax.fori_loop(0, pieces * count, sort_row, (jnp.int32(0), jnp.int32(0)))

    for which in range(2):
        load[which].wait()

        @pl.loop(0, (totals[which] + TILE - 1) // TILE)
        def _(tile):
            base = tile * TILE
            present = jnp.minimum(totals[which] - base, TILE)

            @pl.loop(0, present)
            def _(q):
                row = members[which, base + q]
                place = pl.ds(pl.multiple_of(q * SH, SH), SH)
                image = centred[pl.ds(pl.multiple_of(row * HALVES, HALVES), HALVES), :]
                for t in range(KF // LANES):
                    at = slice(t * LANES, (t + 1) * LANES)
                    to = slice(KF + t * LANES, KF + (t + 1) * LANES)
                    re = jnp.broadcast_to(image[t:t + 1, :], (SH, LANES))
                    im = jnp.broadcast_to(image[HALVES // 2 + t:HALVES // 2 + t + 1, :], (SH, LANES))
                    cosine, sine = cos_ref[:, at], sin_ref[:, at]
                    shifted[place, at] = (re * cosine + im * sine).astype(jnp.bfloat16)
                    shifted[place, to] = (im * cosine - re * sine).astype(jnp.bfloat16)

            scores[...] = lax.dot_general(
                shifted[...], panels[which], (((1,), (1,)), ((), ())),
                preferred_element_type=jnp.float32,
            )

            @pl.loop(0, present)
            def _(q):
                row = members[which, base + q]
                noise = facts[row, 3]
                place = pl.ds(pl.multiple_of(q * SH, SH), SH)
                for b in range(out_ref.shape[3] // BLOCK):
                    at = slice(b * BLOCK, (b + 1) * BLOCK)
                    allowed = facts[row, 4 + first_block + b]
                    term = jnp.minimum(jnp.exp(scores[place, at] * noise), BF16_MAX)
                    out_ref[row // count, row % count, :, at] = (term * allowed).astype(jnp.bfloat16)


def score(me, rows, own_panel, other_panel, cosine, sine):
    pieces, count, _ = rows.shape
    depth = own_panel.shape[0]
    total = pieces * count
    return pl.pallas_call(
        score_kernel,
        out_shape=jax.ShapeDtypeStruct((pieces, count, SH, depth), jnp.bfloat16),
        in_specs=[
            pl.BlockSpec(memory_space=pltpu.SMEM),
            pl.BlockSpec(memory_space=pltpu.VMEM),
            pl.BlockSpec(memory_space=pl.ANY),
            pl.BlockSpec(memory_space=pl.ANY),
            pl.BlockSpec(memory_space=pltpu.VMEM),
            pl.BlockSpec(memory_space=pltpu.VMEM),
        ],
        out_specs=pl.BlockSpec(memory_space=pltpu.VMEM),
        scratch_shapes=[
            pltpu.VMEM((total * HALVES, LANES), jnp.float32),
            pltpu.VMEM((2, depth, 2 * KF), jnp.bfloat16),
            pltpu.VMEM((TILE * SH, 2 * KF), jnp.bfloat16),
            pltpu.VMEM((TILE * SH, depth), jnp.float32),
            pltpu.VMEM((total, LANES), jnp.float32),
            pltpu.SMEM((total, LANES), jnp.float32),
            pltpu.SMEM((2, total + TILE), jnp.int32),
            pltpu.SemaphoreType.DMA((2,)),
            pltpu.SemaphoreType.DMA,
        ],
        compiler_params=pltpu.CompilerParams(vmem_limit_bytes=48 * 1024 * 1024),
        name="score",
    )(me, rows, own_panel, other_panel, cosine, sine)


def weigh_kernel(places, chunks, me_ref, *refs):
    parts, (weights_ref, log_ref) = refs[:-2], refs[-2:]
    depth = parts[0].shape[-1]
    count = parts[0].shape[0]
    lane = lax.broadcasted_iota(jnp.int32, log_ref.shape, 1)
    logs = jnp.zeros(log_ref.shape, jnp.float32)
    for j in range(chunks):
        def one(p, logs, j=j):
            terms = [parts[j * places + s][p].astype(jnp.float32) for s in range(places)]
            total = sum(terms)
            mean = jnp.sum(total, keepdims=True) / (SH * J)
            for s in range(places):
                at = pl.multiple_of(lax.rem(me_ref[2] + s, places) * depth, depth)
                weights_ref[j * count + p, :, pl.ds(at, depth)] = terms[s] / mean
            return jnp.where(lane == j * count + p, jnp.log(mean), logs)

        logs = lax.fori_loop(0, count, one, logs)
    log_ref[...] = logs


def weigh(me, parts, places, chunks):
    count, _, depth = parts[0].shape
    rows = chunks * count
    return pl.pallas_call(
        functools.partial(weigh_kernel, places, chunks),
        out_shape=(
            jax.ShapeDtypeStruct((rows, SH, J), jnp.float32),
            jax.ShapeDtypeStruct((1, rows), jnp.float32),
        ),
        in_specs=[pl.BlockSpec(memory_space=pltpu.SMEM)]
        + [pl.BlockSpec(memory_space=pltpu.VMEM)] * len(parts),
        out_specs=(
            pl.BlockSpec(memory_space=pltpu.VMEM),
            pl.BlockSpec(memory_space=pltpu.VMEM),
        ),
        compiler_params=pltpu.CompilerParams(vmem_limit_bytes=32 * 1024 * 1024),
        name="weigh",
    )(me, *parts)


def block_mask(chosen):
    labels = jnp.arange(NB, dtype=jnp.int32)
    return jnp.max((chosen[:, :, None] == labels[None, None, :]).astype(jnp.bfloat16), axis=1)


def per_device(particles, classes, windows, pose_lists, inverse_noise, projections):
    owners = lax.axis_size("cls")
    places = lax.axis_size("proj")
    pairs = owners // 2
    label, place = lax.axis_index("cls"), lax.axis_index("proj")
    own_x = label // 2
    depth = projections.shape[1]
    me = jnp.stack([label, place * (depth // BLOCK), place]).astype(jnp.int32)

    def along_x(value, by):
        return lax.ppermute(
            value, "cls", [(i, (i + 2 * by) % owners) for i in range(owners)]
        )

    def along_z(value, by):
        return lax.ppermute(
            value, "proj", [(i, (i + by) % places) for i in range(places)]
        )

    rows = jnp.concatenate(
        [
            particles,
            classes.astype(jnp.bfloat16),
            windows.astype(jnp.bfloat16),
            inverse_noise[:, None],
            block_mask(pose_lists),
            jnp.zeros((particles.shape[0], LANES - NB - 4), jnp.bfloat16),
        ],
        axis=1,
    )
    count = rows.shape[0] // CHUNKS
    cosine, sine = (jnp.asarray(table) for table in relative_tables())
    own_panel = projections[0]
    other_panel = lax.ppermute(own_panel, "cls", [(i, i ^ 1) for i in range(owners)])

    parts = []
    for j in range(CHUNKS):
        mine = rows[j * count:(j + 1) * count]
        column = jnp.stack([mine] + [along_z(mine, s) for s in range(1, places)])
        far = [along_x(column, f) for f in range(1, pairs)]
        far_terms = [
            along_x(score(me, far[f - 1], own_panel, other_panel, cosine, sine), -f)
            for f in range(1, pairs)
        ]
        merged = score(me, column, own_panel, other_panel, cosine, sine)
        owner_x = column[:, :, 2 * KF].astype(jnp.int32) // 2
        for f in range(1, pairs):
            there = owner_x == (own_x + f) % pairs
            merged = jnp.where(there[:, :, None, None], far_terms[f - 1], merged)
        parts += [merged[0]] + [along_z(merged[s], -s) for s in range(1, places)]
    posterior, logs = weigh(me, parts, places, CHUNKS)
    return posterior, logs.reshape(-1)


def solution(mesh):
    placed = (
        P(("groups", "cls", "proj"), None),
        P(("groups", "cls", "proj"), None),
        P(("groups", "cls", "proj"), None),
        P(("groups", "cls", "proj"), None),
        P(("groups", "cls", "proj")),
        P("cls", "proj", None),
    )
    return jax.shard_map(
        per_device,
        mesh=mesh,
        in_specs=placed,
        out_specs=(P(("groups", "cls", "proj"), None, None), P(("groups", "cls", "proj"))),
        check_vma=False,
    )
```

time: 417 us -> 103 us (0.25)
  the two profiles are of different devices: /device:TPU:0 before, /device:TPU:12 now
where the time goes in v1:
time: 103 us; the launch traced here: 102 us
  waiting for transfers between devices  55.2 us (54%)
  starting transfers between devices  17.6 us (17%)
  Pallas kernels  17.3 us (17%)
  local copies, waits for them, and re-layouts  8.98 us (9%)
  other arithmetic  1.93 us (2%)
    ppermute x6, waiting for transfers between devices, along_z(): lax.ppermute(value, 'proj', [(i, (i + by) % places) for i in range(places)])  30 us
    ppermute x2, waiting for transfers between devices, along_x(): lax.ppermute(value, 'cls', [(i, (i + 2 * by) % owners) for i in range(own...  25.2 us
    pallas_call x2, Pallas kernels, score(): pl.pallas_call(score_kernel, out_shape=jax.ShapeDtypeStruct((pieces, coun...  13.2 us
    ppermute x6, starting transfers between devices, along_z(): lax.ppermute(value, 'proj', [(i, (i + by) % places) for i in range(places)])  9.88 us
    ppermute x2, starting transfers between devices, along_x(): lax.ppermute(value, 'cls', [(i, (i + 2 * by) % owners) for i in range(own...  7.6 us
    unnamed x13, local copies, waits for them, and re-layouts  6.95 us
    pallas_call x1, Pallas kernels, weigh(): pl.pallas_call(functools.partial(weigh_kernel, places, chunks), out_shape...  4.19 us
  transfers between devices with their start and end apart: 9, of which 8 were waited for; matrix products, arithmetic and copies ran while one was open for 4% of the time, Pallas kernels for 6%

profile of v1, /device:TPU:12, one launch (start us, length us, event | category | flops | bytes accessed | tf_op | source)
XLA Modules:
  0.0 101.7 jit_solution(2311499086182210421)
XLA Ops:
  0.6 0.1 collective-permute-start.4
  0.7 0.7 convert_element_type.19
  1.4 0.7 convert_element_type.20
  2.1 0.1 copy.20
  2.2 0.1 copy.19
  2.2 0.7 copy.21
  3.0 0.8 copy.18
  3.8 0.1 fusion.1
  3.9 1.0 concatenate.3
  4.9 0.5 collective-permute-start.2
  5.3 2.6 %collective-permute-start.1 = (bf16[16,4224]{1,0:T(8,128)(2,1)S(1)}, bf16[16,4224]{1,0:T(8,128)(2,1)S(1)}, u32[]{:S(2)}, u32[]{:S(2)}) collective-permute-start(bf16[16,4224]{1,0:T(8,128)(2,1)S(1)} %concatenate.3), channel_id=1, source_target_pairs={{0,2},{1,3},{2,0},{3,1},{4,6},{5,7},{6,4},{7,5},{8,10},{9,11},{10,... | collective-permute-start | bytes 405512 | tf_op jit(solution)/shard_map/ppermute | solution.py:221
  7.9 2.5 %collective-permute-start = (bf16[16,4224]{1,0:T(8,128)(2,1)S(1)}, bf16[16,4224]{1,0:T(8,128)(2,1)S(1)}, u32[]{:S(2)}, u32[]{:S(2)}) collective-permute-start(bf16[16,4224]{1,0:T(8,128)(2,1)S(1)} %concatenate.3), channel_id=1, source_target_pairs={{0,1},{1,2},{2,3},{3,0},{4,5},{5,6},{6,7},{7,4},{8,9},{9,10},{10,1... | collective-permute-start | bytes 405512 | tf_op jit(solution)/shard_map/ppermute | solution.py:221
  10.4 0.5 collective-permute-done.2
  10.9 6.8 %collective-permute-done.1 = bf16[16,4224]{1,0:T(8,128)(2,1)S(1)} collective-permute-done((bf16[16,4224]{1,0:T(8,128)(2,1)S(1)}, bf16[16,4224]{1,0:T(8,128)(2,1)S(1)}, u32[]{:S(2)}, u32[]{:S(2)}) %collective-permute-start.1) | collective-permute-done | bytes 135200 | tf_op jit(solution)/shard_map/ppermute | solution.py:221
  17.7 2.2 %collective-permute-done = bf16[16,4224]{1,0:T(8,128)(2,1)S(1)} collective-permute-done((bf16[16,4224]{1,0:T(8,128)(2,1)S(1)}, bf16[16,4224]{1,0:T(8,128)(2,1)S(1)}, u32[]{:S(2)}, u32[]{:S(2)}) %collective-permute-start) | collective-permute-done | bytes 135200 | tf_op jit(solution)/shard_map/ppermute | solution.py:221
  19.9 0.1 pad_maximum_fusion.rows_ref
  20.0 1.6 %collective-permute-start.3 = (bf16[4,16,4224]{2,1,0:T(8,128)(2,1)S(1)}, bf16[4,16,4224]{2,1,0:T(8,128)(2,1)S(1)}, u32[]{:S(2)}, u32[]{:S(2)}) collective-permute-start(bf16[4,16,4224]{2,1,0:T(8,128)(2,1)S(1)} %pad_maximum_fusion.rows_ref), channel_id=1, source_target_pairs={{0,8},{4,12},{8,0},{12,4},{1,9},{5,13},{9,1},{13,5},{2,10},{6,14},... | collective-permute-start | bytes 1622024 | tf_op jit(solution)/shard_map/ppermute | solution.py:216
  21.5 0.1 pad_add_fusion.me_ref
  21.6 12.0 %collective-permute-done.3.rows_ref = bf16[4,16,4224]{2,1,0:T(8,128)(2,1)S(1)} collective-permute-done((bf16[4,16,4224]{2,1,0:T(8,128)(2,1)S(1)}, bf16[4,16,4224]{2,1,0:T(8,128)(2,1)S(1)}, u32[]{:S(2)}, u32[]{:S(2)}) %collective-permute-start.3) | collective-permute-done | bytes 540704 | tf_op jit(solution)/shard_map/ppermute | solution.py:216
  33.6 0.0 collective-permute-done.4.other_hbm
  33.6 0.0 copy-start
  33.6 2.2 %copy-done = bf16[1,512,4096]{2,1,0:T(8,128)(2,1)S(1)} copy-done((bf16[1,512,4096]{2,1,0:T(8,128)(2,1)S(1)}, bf16[1,512,4096]{2,1,0:T(8,128)(2,1)}, u32[]{:S(2)}) %copy-start) | copy-done | bytes 4194328
  35.8 0.0 copy-start.2
  35.8 0.9 copy-done.2
  36.7 0.0 copy-start.4
  36.7 0.9 copy-done.4
  37.6 0.0 copy-start.3
  37.6 0.0 copy-start.5
  37.6 6.7 %score.2 = bf16[4,16,16,512]{3,2,1,0:T(8,128)(2,1)S(1)} custom-call(s32[3]{0:T(128)S(1)} %pad_add_fusion.me_ref, bf16[4,16,4224]{2,1,0:T(8,128)(2,1)S(1)} %collective-permute-done.3.rows_ref, bf16[512,4096]{1,0:T(8,128)(2,1)S(1)} %bitcast.19, bf16[512,4096]{1,0:T(8,128)(2,1)} %collective-permute-done.4.other_hbm, f32[16,2048]{1,0:T(8,128)S(1)} %copy-done.4, ...), custom_call_target="tpu_custom_call" | custom-call | tf_op jit(solution)/shard_map/score/pallas_call | solution.py:133
  44.4 6.0 %collective-permute-start.5 = (bf16[4,16,16,512]{3,2,1,0:T(8,128)(2,1)S(1)}, bf16[4,16,16,512]{3,2,1,0:T(8,128)(2,1)S(1)}, u32[]{:S(2)}, u32[]{:S(2)}) collective-permute-start(bf16[4,16,16,512]{3,2,1,0:T(8,128)(2,1)S(1)} %score.2), channel_id=1, source_target_pairs={{0,8},{4,12},{8,0},{12,4},{1,9},{5,13},{9,1},{13,5},{2,10},{6,14},... | collective-permute-start | bytes 3145736 | tf_op jit(solution)/shard_map/ppermute | solution.py:216
  50.4 0.1 convert_reduce_fusion
  50.6 0.0 copy-done.3
  50.6 0.0 copy-done.5
  50.6 0.0 copy-start.1
  50.6 2.2 %copy-done.1 = bf16[1,512,4096]{2,1,0:T(8,128)(2,1)S(1)} copy-done((bf16[1,512,4096]{2,1,0:T(8,128)(2,1)S(1)}, bf16[1,512,4096]{2,1,0:T(8,128)(2,1)}, u32[]{:S(2)}) %copy-start.1) | copy-done | bytes 4194328
  52.8 6.4 %score.3 = bf16[4,16,16,512]{3,2,1,0:T(8,128)(2,1)S(1)} custom-call(s32[3]{0:T(128)S(1)} %pad_add_fusion.me_ref, bf16[4,16,4224]{2,1,0:T(8,128)(2,1)S(1)} %pad_maximum_fusion.rows_ref, bf16[512,4096]{1,0:T(8,128)(2,1)S(1)} %bitcast.20, bf16[512,4096]{1,0:T(8,128)(2,1)} %collective-permute-done.4.other_hbm, f32[16,2048]{1,0:T(8,128)S(1)} %copy-done.5, ...), custom_call_target="tpu_custom_call" | custom-call | tf_op jit(solution)/shard_map/score/pallas_call | solution.py:133
  59.2 13.2 %collective-permute-done.5 = bf16[4,16,16,512]{3,2,1,0:T(8,128)(2,1)S(1)} collective-permute-done((bf16[4,16,16,512]{3,2,1,0:T(8,128)(2,1)S(1)}, bf16[4,16,16,512]{3,2,1,0:T(8,128)(2,1)S(1)}, u32[]{:S(2)}, u32[]{:S(2)}) %collective-permute-start.5) | collective-permute-done | bytes 1048608 | tf_op jit(solution)/shard_map/ppermute | solution.py:216
  72.4 0.2 broadcast_select_fusion
  72.6 0.1 slice_bitcast_fusion
  72.7 2.5 %collective-permute-start.8 = (bf16[16,16,512]{2,1,0:T(8,128)(2,1)S(1)}, bf16[16,16,512]{2,1,0:T(8,128)(2,1)S(1)}, u32[]{:S(2)}, u32[]{:S(2)}) collective-permute-start(bf16[16,16,512]{2,1,0:T(8,128)(2,1)S(1)} %get-tuple-element.6), channel_id=1, source_target_pairs={{0,1},{1,2},{2,3},{3,0},{4,5},{5,6},{6,7},{7,4},{8,9},{9,10},{10,1... | collective-permute-start | bytes 786440 | tf_op jit(solution)/shard_map/ppermute | solution.py:221
  75.2 1.8 %collective-permute-start.7 = (bf16[16,16,512]{2,1,0:T(8,128)(2,1)S(1)}, bf16[16,16,512]{2,1,0:T(8,128)(2,1)S(1)}, u32[]{:S(2)}, u32[]{:S(2)}) collective-permute-start(bf16[16,16,512]{2,1,0:T(8,128)(2,1)S(1)} %get-tuple-element.7), channel_id=1, source_target_pairs={{0,2},{1,3},{2,0},{3,1},{4,6},{5,7},{6,4},{7,5},{8,10},{9,11},{10,... | collective-permute-start | bytes 786440 | tf_op jit(solution)/shard_map/ppermute | solution.py:221
  77.0 0.0 collective-permute-start.6
  77.0 15.9 %collective-permute-done.8.refs_3_ = bf16[16,16,512]{2,1,0:T(8,128)(2,1)S(1)} collective-permute-done((bf16[16,16,512]{2,1,0:T(8,128)(2,1)S(1)}, bf16[16,16,512]{2,1,0:T(8,128)(2,1)S(1)}, u32[]{:S(2)}, u32[]{:S(2)}) %collective-permute-start.8) | collective-permute-done | bytes 262176 | tf_op jit(solution)/shard_map/ppermute | solution.py:221
  92.9 2.9 %collective-permute-done.7.refs_2_ = bf16[16,16,512]{2,1,0:T(8,128)(2,1)S(1)} collective-permute-done((bf16[16,16,512]{2,1,0:T(8,128)(2,1)S(1)}, bf16[16,16,512]{2,1,0:T(8,128)(2,1)S(1)}, u32[]{:S(2)}, u32[]{:S(2)}) %collective-permute-start.7) | collective-permute-done | bytes 262176 | tf_op jit(solution)/shard_map/ppermute | solution.py:221
  95.8 1.7 %collective-permute-done.6.refs_1_ = bf16[16,16,512]{2,1,0:T(8,128)(2,1)S(1)} collective-permute-done((bf16[16,16,512]{2,1,0:T(8,128)(2,1)S(1)}, bf16[16,16,512]{2,1,0:T(8,128)(2,1)S(1)}, u32[]{:S(2)}, u32[]{:S(2)}) %collective-permute-start.6) | collective-permute-done | bytes 262176 | tf_op jit(solution)/shard_map/ppermute | solution.py:221
  97.5 4.2 %weigh.1 = (f32[16,16,2048]{2,1,0:T(8,128)}, f32[1,16]{1,0:T(1,128)}) custom-call(s32[3]{0:T(128)S(1)} %pad_add_fusion.me_ref, bf16[16,16,512]{2,1,0:T(8,128)(2,1)S(1)} %get-tuple-element.9.refs_0_, bf16[16,16,512]{2,1,0:T(8,128)(2,1)S(1)} %collective-permute-done.6.refs_1_, bf16[16,16,512]{2,1,0:T(8,128)(2,1)S(1)} %collective-permute-done.7.refs_2_, ...), custom_call_target="tpu_custom_call" | custom-call | tf_op jit(solution)/shard_map/weigh/pallas_call | solution.py:184
  (2 shorter events, 0.0 us)
Async XLA Ops:
  0.6 33.0 %collective-permute-start.4 = (bf16[512,4096]{1,0:T(8,128)(2,1)}, bf16[512,4096]{1,0:T(8,128)(2,1)}, u32[]{:S(2)}, u32[]{:S(2)}) collective-permute-start(bf16[512,4096]{1,0:T(8,128)(2,1)} %bitcast.18), channel_id=1, source_target_pairs={{0,4},{4,0},{8,12},{12,8},{1,5},{5,1},{9,13},{13,9},{2,6},{6,2},{1... | collective-permute-start | bytes 12582920 | tf_op jit(solution)/shard_map/ppermute | solution.py:239
  4.9 6.0 %collective-permute-start.2 = (bf16[16,4224]{1,0:T(8,128)(2,1)S(1)}, bf16[16,4224]{1,0:T(8,128)(2,1)S(1)}, u32[]{:S(2)}, u32[]{:S(2)}) collective-permute-start(bf16[16,4224]{1,0:T(8,128)(2,1)S(1)} %concatenate.3), channel_id=1, source_target_pairs={{0,3},{1,0},{2,1},{3,2},{4,7},{5,4},{6,5},{7,6},{8,11},{9,8},{10,9... | collective-permute-start | bytes 405512 | tf_op jit(solution)/shard_map/ppermute | solution.py:221
  5.3 12.4 %collective-permute-start.1 = (bf16[16,4224]{1,0:T(8,128)(2,1)S(1)}, bf16[16,4224]{1,0:T(8,128)(2,1)S(1)}, u32[]{:S(2)}, u32[]{:S(2)}) collective-permute-start(bf16[16,4224]{1,0:T(8,128)(2,1)S(1)} %concatenate.3), channel_id=1, source_target_pairs={{0,2},{1,3},{2,0},{3,1},{4,6},{5,7},{6,4},{7,5},{8,10},{9,11},{10,... | collective-permute-start | bytes 405512 | tf_op jit(solution)/shard_map/ppermute | solution.py:221
  7.9 12.0 %collective-permute-start = (bf16[16,4224]{1,0:T(8,128)(2,1)S(1)}, bf16[16,4224]{1,0:T(8,128)(2,1)S(1)}, u32[]{:S(2)}, u32[]{:S(2)}) collective-permute-start(bf16[16,4224]{1,0:T(8,128)(2,1)S(1)} %concatenate.3), channel_id=1, source_target_pairs={{0,1},{1,2},{2,3},{3,0},{4,5},{5,6},{6,7},{7,4},{8,9},{9,10},{10,1... | collective-permute-start | bytes 405512 | tf_op jit(solution)/shard_map/ppermute | solution.py:221
  20.0 13.6 %collective-permute-start.3 = (bf16[4,16,4224]{2,1,0:T(8,128)(2,1)S(1)}, bf16[4,16,4224]{2,1,0:T(8,128)(2,1)S(1)}, u32[]{:S(2)}, u32[]{:S(2)}) collective-permute-start(bf16[4,16,4224]{2,1,0:T(8,128)(2,1)S(1)} %pad_maximum_fusion.rows_ref), channel_id=1, source_target_pairs={{0,8},{4,12},{8,0},{12,4},{1,9},{5,13},{9,1},{13,5},{2,10},{6,14},... | collective-permute-start | bytes 1622024 | tf_op jit(solution)/shard_map/ppermute | solution.py:216
  33.6 2.2 %copy-start = (bf16[1,512,4096]{2,1,0:T(8,128)(2,1)S(1)}, bf16[1,512,4096]{2,1,0:T(8,128)(2,1)}, u32[]{:S(2)}) copy-start(bf16[1,512,4096]{2,1,0:T(8,128)(2,1)} %param.13) | copy-start | bytes 12582916
  35.8 0.9 copy-start.2
  36.7 0.9 copy-start.4
  37.6 12.9 %copy-start.3 = (f32[16,2048]{1,0:T(8,128)S(1)}, f32[16,2048]{1,0:T(8,128)}, u32[]{:S(2)}) copy-start(f32[16,2048]{1,0:T(8,128)} %constant.52.clone.sin_ref) | copy-start | bytes 393220
  37.6 13.0 %copy-start.5 = (f32[16,2048]{1,0:T(8,128)S(1)}, f32[16,2048]{1,0:T(8,128)}, u32[]{:S(2)}) copy-start(f32[16,2048]{1,0:T(8,128)} %constant.51.clone.cos_ref) | copy-start | bytes 393220
  44.4 28.0 %collective-permute-start.5 = (bf16[4,16,16,512]{3,2,1,0:T(8,128)(2,1)S(1)}, bf16[4,16,16,512]{3,2,1,0:T(8,128)(2,1)S(1)}, u32[]{:S(2)}, u32[]{:S(2)}) collective-permute-start(bf16[4,16,16,512]{3,2,1,0:T(8,128)(2,1)S(1)} %score.2), channel_id=1, source_target_pairs={{0,8},{4,12},{8,0},{12,4},{1,9},{5,13},{9,1},{13,5},{2,10},{6,14},... | collective-permute-start | bytes 3145736 | tf_op jit(solution)/shard_map/ppermute | solution.py:216
  50.6 2.2 %copy-start.1 = (bf16[1,512,4096]{2,1,0:T(8,128)(2,1)S(1)}, bf16[1,512,4096]{2,1,0:T(8,128)(2,1)}, u32[]{:S(2)}) copy-start(bf16[1,512,4096]{2,1,0:T(8,128)(2,1)} %param.13) | copy-start | bytes 12582916
  72.7 20.3 %collective-permute-start.8 = (bf16[16,16,512]{2,1,0:T(8,128)(2,1)S(1)}, bf16[16,16,512]{2,1,0:T(8,128)(2,1)S(1)}, u32[]{:S(2)}, u32[]{:S(2)}) collective-permute-start(bf16[16,16,512]{2,1,0:T(8,128)(2,1)S(1)} %get-tuple-element.6), channel_id=1, source_target_pairs={{0,1},{1,2},{2,3},{3,0},{4,5},{5,6},{6,7},{7,4},{8,9},{9,10},{10,1... | collective-permute-start | bytes 786440 | tf_op jit(solution)/shard_map/ppermute | solution.py:221
  75.2 20.6 %collective-permute-start.7 = (bf16[16,16,512]{2,1,0:T(8,128)(2,1)S(1)}, bf16[16,16,512]{2,1,0:T(8,128)(2,1)S(1)}, u32[]{:S(2)}, u32[]{:S(2)}) collective-permute-start(bf16[16,16,512]{2,1,0:T(8,128)(2,1)S(1)} %get-tuple-element.7), channel_id=1, source_target_pairs={{0,2},{1,3},{2,0},{3,1},{4,6},{5,7},{6,4},{7,5},{8,10},{9,11},{10,... | collective-permute-start | bytes 786440 | tf_op jit(solution)/shard_map/ppermute | solution.py:221
  77.0 20.5 %collective-permute-start.6 = (bf16[16,16,512]{2,1,0:T(8,128)(2,1)S(1)}, bf16[16,16,512]{2,1,0:T(8,128)(2,1)S(1)}, u32[]{:S(2)}, u32[]{:S(2)}) collective-permute-start(bf16[16,16,512]{2,1,0:T(8,128)(2,1)S(1)} %get-tuple-element.8), channel_id=1, source_target_pairs={{0,3},{1,0},{2,1},{3,2},{4,7},{5,4},{6,5},{7,6},{8,11},{9,8},{10,9... | collective-permute-start | bytes 786440 | tf_op jit(solution)/shard_map/ppermute | solution.py:221

commit v2 on v1

v2 whole, which is shorter than its diff:
```python
import functools
import math

import jax
import jax.numpy as jnp
from jax import lax
from jax.experimental import pallas as pl
from jax.experimental.pallas import tpu as pltpu
from jax.sharding import PartitionSpec as P

IMG = 64
KF = 2048
J = 2048
NB = 16
SW = 4
SH = 16
LANES = 128
WIDTH = 2 * KF + LANES
HALVES = 2 * KF // LANES
TILE = 8
TURN = 1024
GROUP = 4
BLOCK = J // NB
CHUNKS = 2
BF16_MAX = float(jnp.finfo(jnp.bfloat16).max)


def unit_circle(turn):
    turn = turn - IMG * jnp.floor(turn * (1.0 / IMG) + 0.5)
    half = turn * (math.pi / IMG)
    square = half * half
    sine, cosine = jnp.zeros_like(half), jnp.zeros_like(half)
    for n in (13, 11, 9, 7, 5, 3, 1):
        sine = sine * square + (-1.0) ** (n // 2) / math.factorial(n)
    for n in (14, 12, 10, 8, 6, 4, 2, 0):
        cosine = cosine * square + (-1.0) ** (n // 2) / math.factorial(n)
    sine = sine * half
    return 1.0 - 2.0 * sine * sine, 2.0 * sine * cosine


def pack_kernel(particles_ref, classes_ref, windows_ref, poses_ref, noise_ref, *refs):
    outs, facts = refs[:-1], refs[-1]
    count = particles_ref.shape[0]
    held = NB + 4 + 4
    line = lax.broadcasted_iota(jnp.int32, (held, count), 0)

    def spread(row):
        return jnp.broadcast_to(row, (held, count))

    column = jnp.where(line == 0, spread(classes_ref[...]).astype(jnp.float32), 0.0)
    column = jnp.where(line == 1, spread(windows_ref[0:1, :]).astype(jnp.float32), column)
    column = jnp.where(line == 2, spread(windows_ref[1:2, :]).astype(jnp.float32), column)
    column = jnp.where(line == 3, spread(noise_ref[...].astype(jnp.float32)), column)
    for n in range(poses_ref.shape[0]):
        column = jnp.where(line == spread(poses_ref[n:n + 1, :]) + 4, 1.0, column)
    facts[...] = jnp.zeros(facts.shape, jnp.float32)
    facts[0:held, 0:count] = column
    tail = facts[...].T[0:count, :].astype(jnp.bfloat16)
    part = count // len(outs)
    for j, out_ref in enumerate(outs):
        out_ref[:, 0:2 * KF] = particles_ref[j * part:(j + 1) * part, :]
        out_ref[:, 2 * KF:] = tail[j * part:(j + 1) * part, :]


def pack(particles, classes, windows, pose_lists, inverse_noise):
    count = particles.shape[0]
    whole = pl.BlockSpec(memory_space=pltpu.VMEM)
    return pl.pallas_call(
        pack_kernel,
        out_shape=[jax.ShapeDtypeStruct((count // CHUNKS, WIDTH), jnp.bfloat16)] * CHUNKS,
        in_specs=[whole] * 5,
        out_specs=[whole] * CHUNKS,
        scratch_shapes=[pltpu.VMEM((LANES, LANES), jnp.float32)],
        name="pack",
    )(particles, classes.T, windows.T, pose_lists.T, inverse_noise[None, :])


def turn_kernel(own_ref, other_ref, own_out, other_out, cos_ref, sin_ref):
    own_out[...] = own_ref[...].T
    other_out[...] = other_ref[...].T

    @pl.when(pl.program_id(0) == 0)
    def _():
        shift = lax.broadcasted_iota(jnp.int32, cos_ref.shape, 0)
        c = lax.broadcasted_iota(jnp.int32, cos_ref.shape, 1)
        kx, ky = c % IMG - IMG // 2, c // IMG
        turn = (shift % SW - SW // 2) * kx + (shift // SW - SW // 2) * ky
        cos_ref[...], sin_ref[...] = unit_circle(turn.astype(jnp.float32))


def turn(own_panel, other_panel):
    depth, width = own_panel.shape
    turned = jax.ShapeDtypeStruct((width, depth), own_panel.dtype)
    table = jax.ShapeDtypeStruct((SH, KF), jnp.float32)
    fixed = pl.BlockSpec((SH, KF), lambda i: (0, 0))
    return pl.pallas_call(
        turn_kernel,
        grid=(width // TURN,),
        out_shape=[turned, turned, table, table],
        in_specs=[pl.BlockSpec((depth, TURN), lambda i: (0, i))] * 2,
        out_specs=[pl.BlockSpec((TURN, depth), lambda i: (i, 0))] * 2 + [fixed] * 2,
        compiler_params=pltpu.CompilerParams(vmem_limit_bytes=20 * 1024 * 1024),
        cost_estimate=pl.CostEstimate(flops=0, bytes_accessed=16 << 20, transcendentals=0),
        name="turn",
    )(own_panel, other_panel)


def score_kernel(
    me_ref, rows_ref, own_any, other_any, cos_ref, sin_ref, out_ref,
    centred, shifted, scores, details, facts, members, panels, fact_sem, panel_sems,
):
    pieces, count, _ = rows_ref.shape
    for s in range(pieces):
        details[s * count:(s + 1) * count, :] = rows_ref[s, :, 2 * KF:].astype(jnp.float32)
    send = pltpu.make_async_copy(details, facts, fact_sem)
    send.start()
    loads = [
        pltpu.make_async_copy(panel, panels.at[n], panel_sems.at[n])
        for n, panel in enumerate((own_any, other_any))
    ]
    for copy in loads:
        copy.start()

    lane = lax.broadcasted_iota(jnp.int32, (count, LANES), 1)
    kx = (lane % IMG - IMG // 2).astype(jnp.float32)
    odd = (lane // IMG).astype(jnp.float32)
    for s in range(pieces):
        fact = details[s * count:(s + 1) * count, :]
        wx = jnp.broadcast_to(fact[:, 1:2], (count, LANES))
        wy = jnp.broadcast_to(fact[:, 2:3], (count, LANES))
        cosine, sine = unit_circle(wx * kx + wy * odd)
        step_cos, step_sin = unit_circle(wy * 2.0)
        for t in range(KF // LANES):
            at = slice(t * LANES, (t + 1) * LANES)
            to = slice(KF + t * LANES, KF + (t + 1) * LANES)
            re = rows_ref[s, :, at].astype(jnp.float32)
            im = rows_ref[s, :, to].astype(jnp.float32)
            centred[pl.ds(s * count * HALVES + t, count, HALVES), :] = re * cosine + im * sine
            centred[pl.ds(s * count * HALVES + HALVES // 2 + t, count, HALVES), :] = im * cosine - re * sine
            cosine, sine = (
                cosine * step_cos - sine * step_sin,
                sine * step_cos + cosine * step_sin,
            )
    send.wait()

    own = me_ref[0].astype(jnp.float32)
    other = (me_ref[0] ^ 1).astype(jnp.float32)
    first_block = me_ref[1]

    def sort_row(row, filled):
        label = facts[row, 0]
        members[0, filled[0]] = row
        members[1, filled[1]] = row
        return (
            filled[0] + (label == own).astype(jnp.int32),
            filled[1] + (label == other).astype(jnp.int32),
        )

    totals = lax.fori_loop(0, pieces * count, sort_row, (jnp.int32(0), jnp.int32(0)))

    for which, copy in enumerate(loads):
        copy.wait()

        @pl.loop(0, (totals[which] + TILE - 1) // TILE)
        def _(tile):
            base = tile * TILE
            present = jnp.minimum(totals[which] - base, TILE)

            spots = []
            for q in range(TILE):
                row = jnp.where(q < present, members[which, base + q], 0)
                spots.append(pl.multiple_of(row * HALVES, HALVES))
            for t in range(KF // LANES):
                at = slice(t * LANES, (t + 1) * LANES)
                to = slice(KF + t * LANES, KF + (t + 1) * LANES)
                cosine, sine = cos_ref[:, at], sin_ref[:, at]
                for q in range(TILE):
                    place = slice(q * SH, (q + 1) * SH)
                    base_re = spots[q] + t // 8 * 8
                    re = centred[pl.ds(pl.multiple_of(base_re, 8), 8), :][t % 8:t % 8 + 1, :]
                    im = centred[pl.ds(pl.multiple_of(base_re + HALVES // 2, 8), 8), :][t % 8:t % 8 + 1, :]
                    re = jnp.broadcast_to(re, (SH, LANES))
                    im = jnp.broadcast_to(im, (SH, LANES))
                    shifted[place, at] = (re * cosine + im * sine).astype(jnp.bfloat16)
                    shifted[place, to] = (im * cosine - re * sine).astype(jnp.bfloat16)

            scores[...] = jnp.dot(shifted[...], panels[which], preferred_element_type=jnp.float32)

            @pl.loop(0, present)
            def _(q):
                row = members[which, base + q]
                noise = facts[row, 3]
                place = pl.ds(pl.multiple_of(q * SH, SH), SH)
                for b in range(out_ref.shape[3] // BLOCK):
                    at = slice(b * BLOCK, (b + 1) * BLOCK)
                    allowed = facts[row, 4 + first_block + b]
                    term = jnp.minimum(jnp.exp(scores[place, at] * noise), BF16_MAX)
                    out_ref[row // count, row % count, :, at] = (term * allowed).astype(jnp.bfloat16)


def score(me, rows, own_panel, other_panel, cosine, sine):
    pieces, count, _ = rows.shape
    depth = own_panel.shape[1]
    total = pieces * count
    return pl.pallas_call(
        score_kernel,
        out_shape=jax.ShapeDtypeStruct((pieces, count, SH, depth), jnp.bfloat16),
        in_specs=[
            pl.BlockSpec(memory_space=pltpu.SMEM),
            pl.BlockSpec(memory_space=pltpu.VMEM),
            pl.BlockSpec(memory_space=pl.ANY),
            pl.BlockSpec(memory_space=pl.ANY),
            pl.BlockSpec(memory_space=pltpu.VMEM),
            pl.BlockSpec(memory_space=pltpu.VMEM),
        ],
        out_specs=pl.BlockSpec(memory_space=pltpu.VMEM),
        scratch_shapes=[
            pltpu.VMEM((total * HALVES, LANES), jnp.float32),
            pltpu.VMEM((TILE * SH, 2 * KF), jnp.bfloat16),
            pltpu.VMEM((TILE * SH, depth), jnp.float32),
            pltpu.VMEM((total, LANES), jnp.float32),
            pltpu.SMEM((total, LANES), jnp.float32),
            pltpu.SMEM((2, total + TILE), jnp.int32),
            pltpu.VMEM((2, 2 * KF, depth), jnp.bfloat16),
            pltpu.SemaphoreType.DMA,
            pltpu.SemaphoreType.DMA((2,)),
        ],
        compiler_params=pltpu.CompilerParams(vmem_limit_bytes=24 * 1024 * 1024),
        cost_estimate=pl.CostEstimate(
            flops=total * SH * depth * 4 * KF, bytes_accessed=16 << 20, transcendentals=0
        ),
        name="score",
    )(me, rows, own_panel, other_panel, cosine, sine)


def weigh_kernel(places, first, me_ref, *refs):
    parts, (weights_ref, log_ref) = refs[:places], refs[-2:]
    group, _, depth = parts[0].shape
    step = pl.program_id(0)

    @pl.when(step == 0)
    def _():
        log_ref[...] = refs[places + 1][...] if first else jnp.zeros(log_ref.shape, jnp.float32)

    lane = lax.broadcasted_iota(jnp.int32, log_ref.shape, 1)
    logs = log_ref[...]
    for g in range(group):
        total = sum(part[g].astype(jnp.float32) for part in parts)
        mean = jnp.sum(total, keepdims=True) / (SH * J)
        scale = 1.0 / mean
        for s in range(places):
            at = pl.multiple_of((me_ref[2] ^ s) * depth, depth)
            weights_ref[g, :, pl.ds(at, depth)] = parts[s][g].astype(jnp.float32) * scale
        logs = jnp.where(lane == first + step * group + g, jnp.log(mean), logs)
    log_ref[...] = logs


def weigh(me, parts, first, rows, before):
    places = len(parts)
    count, _, depth = parts[0].shape
    group = min(GROUP, count)
    logs = pl.BlockSpec((1, rows), lambda i: (0, 0))
    return pl.pallas_call(
        functools.partial(weigh_kernel, places, first),
        grid=(count // group,),
        out_shape=(
            jax.ShapeDtypeStruct((rows, SH, J), jnp.float32),
            jax.ShapeDtypeStruct((1, rows), jnp.float32),
        ),
        in_specs=[pl.BlockSpec(memory_space=pltpu.SMEM)]
        + [pl.BlockSpec((group, SH, depth), lambda i: (i, 0, 0))] * places
        + [pl.BlockSpec(memory_space=pl.ANY), logs][:len(before)],
        out_specs=(pl.BlockSpec((group, SH, J), lambda i: (first // group + i, 0, 0)), logs),
        input_output_aliases={places + 1: 0} if before else {},
        compiler_params=pltpu.CompilerParams(vmem_limit_bytes=16 * 1024 * 1024),
        name="weigh",
    )(me, *parts, *before)


def per_device(particles, classes, windows, pose_lists, inverse_noise, projections):
    owners = lax.axis_size("cls")
    places = lax.axis_size("proj")
    pairs = owners // 2
    label, place = lax.axis_index("cls"), lax.axis_index("proj")
    own_x = label // 2
    depth = projections.shape[1]
    me = jnp.stack([label, place * (depth // BLOCK), place]).astype(jnp.int32)

    def along_x(value, by):
        return lax.ppermute(value, "cls", [(i, i ^ (2 * by)) for i in range(owners)])

    def along_z(value, by):
        return lax.ppermute(value, "proj", [(i, i ^ by) for i in range(places)])

    chunks = pack(particles, classes, windows, pose_lists, inverse_noise)
    pieces = [[mine] + [along_z(mine, s) for s in range(1, places)] for mine in chunks]
    other_panel = lax.ppermute(projections[0], "cls", [(i, i ^ 1) for i in range(owners)])
    panels = turn(projections[0], other_panel)
    panels, pieces[1] = lax.optimization_barrier((panels, pieces[1]))
    columns = [jnp.stack(piece) for piece in pieces]
    far = [[along_x(column, f) for f in range(1, pairs)] for column in columns]
    near_terms = [score(me, columns[0], *panels)]
    far[0], near_terms[0], columns[1:] = lax.optimization_barrier((far[0], near_terms[0], columns[1:]))
    far_terms = []
    for group in far:
        terms = [score(me, rows, *panels) for rows in group]
        far_terms.append([along_x(t, f + 1) for f, t in enumerate(terms)])
    for column in columns[1:]:
        column, _ = lax.optimization_barrier((column, terms))
        near_terms.append(score(me, column, *panels))
    done = ()
    for j, column in enumerate(columns):
        if j:
            far_terms[j], parts = lax.optimization_barrier((far_terms[j], parts))
            done = weigh(me, parts, (j - 1) * column.shape[1], particles.shape[0], done)
        merged = near_terms[j]
        owner_x = column[:, :, 2 * KF].astype(jnp.int32) // 2
        for f in range(1, pairs):
            there = owner_x == (own_x ^ f)
            merged = jnp.where(there[:, :, None, None], far_terms[j][f - 1], merged)
        parts = [merged[0]] + [along_z(merged[s], s) for s in range(1, places)]
    done = weigh(me, parts, (CHUNKS - 1) * column.shape[1], particles.shape[0], done)
    return done[0], done[1].reshape(-1)


def solution(mesh):
    placed = (
        P(("groups", "cls", "proj"), None),
        P(("groups", "cls", "proj"), None),
        P(("groups", "cls", "proj"), None),
        P(("groups", "cls", "proj"), None),
        P(("groups", "cls", "proj")),
        P("cls", "proj", None),
    )
    return jax.shard_map(
        per_device,
        mesh=mesh,
        in_specs=placed,
        out_specs=(P(("groups", "cls", "proj"), None, None), P(("groups", "cls", "proj"))),
        check_vma=False,
    )
```

time: 103 us -> 77 us (0.75)
  the two profiles are of different devices: /device:TPU:12 before, /device:TPU:0 now
where the time goes in v2:
time: 77 us; the launch traced here: 75.8 us
  Pallas kernels  32.4 us (42%)
  starting transfers between devices  22.1 us (29%)
  waiting for transfers between devices  16.6 us (22%)
  local copies, waits for them, and re-layouts  2.26 us (3%)
  other arithmetic  1.64 us (2%)
  between operations  0.83 us (1%)
    pallas_call x4, Pallas kernels, score(): pl.pallas_call(score_kernel, out_shape=jax.ShapeDtypeStruct((pieces, coun...  22.5 us
    ppermute x12, starting transfers between devices, along_z(): return lax.ppermute(value, 'proj', [(i, i ^ by) for i in range(places)])  19.3 us
    ppermute x4, waiting for transfers between devices, along_x(): return lax.ppermute(value, 'cls', [(i, i ^ 2 * by) for i in range(owners)])  8.71 us
    ppermute x12, waiting for transfers between devices, along_z(): return lax.ppermute(value, 'proj', [(i, i ^ by) for i in range(places)])  7.84 us
    pallas_call x1, Pallas kernels, turn(): pl.pallas_call(turn_kernel, grid=(width // TURN,), out_shape=[turned, tur...  4.78 us
    pallas_call x2, Pallas kernels, weigh(): pl.pallas_call(functools.partial(weigh_kernel, places, first), grid=(coun...  3.47 us
    ppermute x4, starting transfers between devices, along_x(): return lax.ppermute(value, 'cls', [(i, i ^ 2 * by) for i in range(owners)])  2.36 us
    unnamed x4, local copies, waits for them, and re-layouts  2.19 us
  transfers between devices with their start and end apart: 17, of which 5 were waited for; matrix products, arithmetic and copies ran while one was open for 2% of the time, Pallas kernels for 40%

profile of v2, /device:TPU:0, one launch (start us, length us, event | category | flops | bytes accessed | tf_op | source)
XLA Modules:
  0.0 75.8 jit_solution(12899692810475062673)
XLA Ops:
  0.6 0.5 collective-permute-start.4
  1.1 1.7 %pack.1 = (bf16[8,4224]{1,0:T(8,128)(2,1)}, bf16[8,4224]{1,0:T(8,128)(2,1)}) custom-call(bf16[16,4096]{1,0:T(8,128)(2,1)} %particles_ref.1, s32[1,16]{1,0:T(1,128)} %bitcast.45, s32[2,16]{1,0:T(2,128)} %bitcast.44, s32[8,16]{1,0:T(8,128)} %bitcast.43, bf16[1,16]{1,0:T(2,128)(2,1)} %bitcast.46), custom_call_target="tpu_custom_call" | custom-call | tf_op jit(solution)/shard_map/pack/pallas_call | solution.py:68
  2.8 4.6 %collective-permute-start.2 = (bf16[8,4224]{1,0:T(8,128)(2,1)}, bf16[8,4224]{1,0:T(8,128)(2,1)S(1)}, u32[]{:S(2)}, u32[]{:S(2)}) collective-permute-start(bf16[8,4224]{1,0:T(8,128)(2,1)} %get-tuple-element.29), channel_id=1, source_target_pairs={{0,3},{1,2},{2,1},{3,0},{4,7},{5,6},{6,5},{7,4},{8,11},{9,10},{10,... | collective-permute-start | bytes 202760 | tf_op jit(solution)/shard_map/ppermute | solution.py:293
  7.4 0.0 collective-permute-start
  7.4 0.6 collective-permute-start.1
  8.0 1.5 %collective-permute-start.5 = (bf16[8,4224]{1,0:T(8,128)(2,1)}, bf16[8,4224]{1,0:T(8,128)(2,1)S(1)}, u32[]{:S(2)}, u32[]{:S(2)}) collective-permute-start(bf16[8,4224]{1,0:T(8,128)(2,1)} %get-tuple-element.39), channel_id=1, source_target_pairs={{0,1},{1,0},{2,3},{3,2},{4,5},{5,4},{6,7},{7,6},{8,9},{9,8},{10,11... | collective-permute-start | bytes 202760 | tf_op jit(solution)/shard_map/ppermute | solution.py:293
  9.5 0.1 pad_add_fusion.me_ref
  9.5 1.1 %collective-permute-done.2 = bf16[8,4224]{1,0:T(8,128)(2,1)S(1)} collective-permute-done((bf16[8,4224]{1,0:T(8,128)(2,1)}, bf16[8,4224]{1,0:T(8,128)(2,1)S(1)}, u32[]{:S(2)}, u32[]{:S(2)}) %collective-permute-start.2) | collective-permute-done | bytes 67616 | tf_op jit(solution)/shard_map/ppermute | solution.py:293
  10.7 1.8 %collective-permute-start.6 = (bf16[8,4224]{1,0:T(8,128)(2,1)}, bf16[8,4224]{1,0:T(8,128)(2,1)S(1)}, u32[]{:S(2)}, u32[]{:S(2)}) collective-permute-start(bf16[8,4224]{1,0:T(8,128)(2,1)} %get-tuple-element.39), channel_id=1, source_target_pairs={{0,2},{1,3},{2,0},{3,1},{4,6},{5,7},{6,4},{7,5},{8,10},{9,11},{10,... | collective-permute-start | bytes 202760 | tf_op jit(solution)/shard_map/ppermute | solution.py:293
  12.5 1.6 %collective-permute-done = bf16[8,4224]{1,0:T(8,128)(2,1)S(1)} collective-permute-done((bf16[8,4224]{1,0:T(8,128)(2,1)}, bf16[8,4224]{1,0:T(8,128)(2,1)S(1)}, u32[]{:S(2)}, u32[]{:S(2)}) %collective-permute-start) | collective-permute-done | bytes 67616 | tf_op jit(solution)/shard_map/ppermute | solution.py:293
  14.1 0.3 collective-permute-start.7
  14.4 0.0 collective-permute-done.1
  14.4 0.9 %pad_maximum_fusion.rows_ref = bf16[4,8,4224]{2,1,0:T(8,128)(2,1)S(1)} fusion(bf16[1,8,4224]{2,1,0:T(8,128)(2,1)S(1)} %bitcast.38, bf16[1,8,4224]{2,1,0:T(8,128)(2,1)S(1)} %bitcast.40, bf16[1,8,4224]{2,1,0:T(8,128)(2,1)S(1)} %bitcast.39, bf16[1,8,4224]{2,1,0:T(8,128)(2,1)} %bitcast.37), kind=kLoop, calls=%fused_computation.2 | loop fusion | flops 405504 | bytes 540672 | tf_op jit(solution)/shard_map/stack | solution.py:300
  15.3 1.6 %collective-permute-start.3 = (bf16[4,8,4224]{2,1,0:T(8,128)(2,1)S(1)}, bf16[4,8,4224]{2,1,0:T(8,128)(2,1)S(1)}, u32[]{:S(2)}, u32[]{:S(2)}) collective-permute-start(bf16[4,8,4224]{2,1,0:T(8,128)(2,1)S(1)} %pad_maximum_fusion.rows_ref), channel_id=1, source_target_pairs={{0,8},{4,12},{8,0},{12,4},{1,9},{5,13},{9,1},{13,5},{2,10},{6,14},... | collective-permute-start | bytes 811016 | tf_op jit(solution)/shard_map/ppermute | solution.py:290
  16.9 0.1 convert_reduce_fusion
  17.0 0.0 collective-permute-done.4.other_ref
  17.1 0.0 copy-start
  17.1 2.2 %copy-done = bf16[1,512,4096]{2,1,0:T(8,128)(2,1)S(1)} copy-done((bf16[1,512,4096]{2,1,0:T(8,128)(2,1)S(1)}, bf16[1,512,4096]{2,1,0:T(8,128)(2,1)}, u32[]{:S(2)}) %copy-start) | copy-done | bytes 4194328
  19.2 4.8 %turn.1 = (bf16[4096,512]{1,0:T(8,128)(2,1)S(1)}, bf16[4096,512]{1,0:T(8,128)(2,1)S(1)}, f32[16,2048]{1,0:T(8,128)S(1)}, f32[16,2048]{1,0:T(8,128)S(1)}) custom-call(bf16[512,4096]{1,0:T(8,128)(2,1)S(1)} %bitcast.34, bf16[512,4096]{1,0:T(8,128)(2,1)} %collective-permute-done.4.other_ref), custom_call_target="tpu_custom_call" | custom-call | bytes 16777216 | tf_op jit(solution)/shard_map/turn/pallas_call | solution.py:96
  24.0 0.0 collective-permute-done.5
  24.0 0.0 collective-permute-done.6
  24.1 0.0 collective-permute-done.7
  24.1 0.6 collective-permute-start.8
  24.7 4.9 %score.4 = bf16[4,8,16,512]{3,2,1,0:T(8,128)(2,1)S(1)} custom-call(s32[3]{0:T(128)S(1)} %pad_add_fusion.me_ref, bf16[4,8,4224]{2,1,0:T(8,128)(2,1)S(1)} %pad_maximum_fusion.rows_ref, bf16[4096,512]{1,0:T(8,128)(2,1)S(1)} %get-tuple-element.35.own_any, bf16[4096,512]{1,0:T(8,128)(2,1)S(1)} %get-tuple-element.36.other_any, ...), custom_call_target="tpu_custom_call" | custom-call | flops 2147483648 | bytes 16777216 | tf_op jit(solution)/shard_map/score/pallas_call | solution.py:205
  29.7 0.0 collective-permute-done.3.rows_ref
  29.7 5.9 %score.6 = bf16[4,8,16,512]{3,2,1,0:T(8,128)(2,1)S(1)} custom-call(s32[3]{0:T(128)S(1)} %pad_add_fusion.me_ref, bf16[4,8,4224]{2,1,0:T(8,128)(2,1)S(1)} %collective-permute-done.3.rows_ref, bf16[4096,512]{1,0:T(8,128)(2,1)S(1)} %get-tuple-element.35.own_any, bf16[4096,512]{1,0:T(8,128)(2,1)S(1)} %get-tuple-element.36.other_any, ...), custom_call_target="tpu_custom_call" | custom-call | flops 2147483648 | bytes 16777216 | tf_op jit(solution)/shard_map/score/pallas_call | solution.py:205
  35.6 0.1 collective-permute-start.10
  35.6 0.1 convert_reduce_fusion.1
  35.8 0.0 collective-permute-done.8.rows_ref
  35.8 5.8 %score.5 = bf16[4,8,16,512]{3,2,1,0:T(8,128)(2,1)S(1)} custom-call(s32[3]{0:T(128)S(1)} %pad_add_fusion.me_ref, bf16[4,8,4224]{2,1,0:T(8,128)(2,1)S(1)} %collective-permute-done.8.rows_ref, bf16[4096,512]{1,0:T(8,128)(2,1)S(1)} %get-tuple-element.35.own_any, bf16[4096,512]{1,0:T(8,128)(2,1)S(1)} %get-tuple-element.36.other_any, ...), custom_call_target="tpu_custom_call" | custom-call | flops 2147483648 | bytes 16777216 | tf_op jit(solution)/shard_map/score/pallas_call | solution.py:205
  41.7 0.1 collective-permute-start.9
  41.8 8.7 %collective-permute-done.10 = bf16[4,8,16,512]{3,2,1,0:T(8,128)(2,1)S(1)} collective-permute-done((bf16[4,8,16,512]{3,2,1,0:T(8,128)(2,1)S(1)}, bf16[4,8,16,512]{3,2,1,0:T(8,128)(2,1)S(1)}, u32[]{:S(2)}, u32[]{:S(2)}) %collective-permute-start.10) | collective-permute-done | bytes 524320 | tf_op jit(solution)/shard_map/ppermute | solution.py:290
  50.5 0.1 broadcast_select_fusion
  50.7 1.0 %collective-permute-start.11 = (bf16[8,16,512]{2,1,0:T(8,128)(2,1)S(1)}, bf16[8,16,512]{2,1,0:T(8,128)(2,1)S(1)}, u32[]{:S(2)}, u32[]{:S(2)}) collective-permute-start(bf16[8,16,512]{2,1,0:T(8,128)(2,1)S(1)} %get-tuple-element.62), channel_id=1, source_target_pairs={{0,1},{1,0},{2,3},{3,2},{4,5},{5,4},{6,7},{7,6},{8,9},{9,8},{10,11... | collective-permute-start | bytes 393224 | tf_op jit(solution)/shard_map/ppermute | solution.py:293
  51.7 3.2 %collective-permute-start.12 = (bf16[8,16,512]{2,1,0:T(8,128)(2,1)S(1)}, bf16[8,16,512]{2,1,0:T(8,128)(2,1)S(1)}, u32[]{:S(2)}, u32[]{:S(2)}) collective-permute-start(bf16[8,16,512]{2,1,0:T(8,128)(2,1)S(1)} %get-tuple-element.61), channel_id=1, source_target_pairs={{0,2},{1,3},{2,0},{3,1},{4,6},{5,7},{6,4},{7,5},{8,10},{9,11},{10,... | collective-permute-start | bytes 393224 | tf_op jit(solution)/shard_map/ppermute | solution.py:293
  54.9 0.3 collective-permute-start.13
  55.1 5.8 %score.7 = bf16[4,8,16,512]{3,2,1,0:T(8,128)(2,1)S(1)} custom-call(s32[3]{0:T(128)S(1)} %pad_add_fusion.me_ref, bf16[4,8,4224]{2,1,0:T(8,128)(2,1)S(1)} %pad_maximum_fusion.1.rows_ref, bf16[4096,512]{1,0:T(8,128)(2,1)S(1)} %get-tuple-element.35.own_any, bf16[4096,512]{1,0:T(8,128)(2,1)S(1)} %get-tuple-element.36.other_any, ...), custom_call_target="tpu_custom_call" | custom-call | flops 2147483648 | bytes 16777216 | tf_op jit(solution)/shard_map/score/pallas_call | solution.py:205
  61.0 0.0 collective-permute-done.11.refs_1_
  61.0 0.0 collective-permute-done.12.refs_2_
  61.0 1.0 %collective-permute-done.13.refs_3_ = bf16[8,16,512]{2,1,0:T(8,128)(2,1)S(1)} collective-permute-done((bf16[8,16,512]{2,1,0:T(8,128)(2,1)S(1)}, bf16[8,16,512]{2,1,0:T(8,128)(2,1)S(1)}, u32[]{:S(2)}, u32[]{:S(2)}) %collective-permute-start.13) | collective-permute-done | bytes 131104 | tf_op jit(solution)/shard_map/ppermute | solution.py:293
  62.0 0.1 broadcast_select_fusion.1
  62.2 0.9 %collective-permute-start.14 = (bf16[8,16,512]{2,1,0:T(8,128)(2,1)S(1)}, bf16[8,16,512]{2,1,0:T(8,128)(2,1)S(1)}, u32[]{:S(2)}, u32[]{:S(2)}) collective-permute-start(bf16[8,16,512]{2,1,0:T(8,128)(2,1)S(1)} %get-tuple-element.58), channel_id=1, source_target_pairs={{0,1},{1,0},{2,3},{3,2},{4,5},{5,4},{6,7},{7,6},{8,9},{9,8},{10,11... | collective-permute-start | bytes 393224 | tf_op jit(solution)/shard_map/ppermute | solution.py:293
  63.1 3.8 %collective-permute-start.15 = (bf16[8,16,512]{2,1,0:T(8,128)(2,1)S(1)}, bf16[8,16,512]{2,1,0:T(8,128)(2,1)S(1)}, u32[]{:S(2)}, u32[]{:S(2)}) collective-permute-start(bf16[8,16,512]{2,1,0:T(8,128)(2,1)S(1)} %get-tuple-element.57), channel_id=1, source_target_pairs={{0,2},{1,3},{2,0},{3,1},{4,6},{5,7},{6,4},{7,5},{8,10},{9,11},{10,... | collective-permute-start | bytes 393224 | tf_op jit(solution)/shard_map/ppermute | solution.py:293
  66.8 1.4 %collective-permute-start.16 = (bf16[8,16,512]{2,1,0:T(8,128)(2,1)S(1)}, bf16[8,16,512]{2,1,0:T(8,128)(2,1)S(1)}, u32[]{:S(2)}, u32[]{:S(2)}) collective-permute-start(bf16[8,16,512]{2,1,0:T(8,128)(2,1)S(1)} %get-tuple-element.56), channel_id=1, source_target_pairs={{0,3},{1,2},{2,1},{3,0},{4,7},{5,6},{6,5},{7,4},{8,11},{9,10},{10,... | collective-permute-start | bytes 393224 | tf_op jit(solution)/shard_map/ppermute | solution.py:293
  68.2 1.7 %weigh.2 = (f32[16,16,2048]{2,1,0:T(8,128)}, f32[1,16]{1,0:T(1,128)S(1)}) custom-call(s32[3]{0:T(128)S(1)} %pad_add_fusion.me_ref, bf16[8,16,512]{2,1,0:T(8,128)(2,1)S(1)} %get-tuple-element.48.refs_0_, bf16[8,16,512]{2,1,0:T(8,128)(2,1)S(1)} %collective-permute-done.11.refs_1_, bf16[8,16,512]{2,1,0:T(8,128)(2,1)S(1)} %collective-permute-done.12.refs_2_, ...), custom_call_target="tpu_custom_call" | custom-call | tf_op jit(solution)/shard_map/weigh/pallas_call | solution.py:263
  70.0 0.0 collective-permute-done.15.refs_2_
  70.0 4.1 %collective-permute-done.16.refs_3_ = bf16[8,16,512]{2,1,0:T(8,128)(2,1)S(1)} collective-permute-done((bf16[8,16,512]{2,1,0:T(8,128)(2,1)S(1)}, bf16[8,16,512]{2,1,0:T(8,128)(2,1)S(1)}, u32[]{:S(2)}, u32[]{:S(2)}) %collective-permute-start.16) | collective-permute-done | bytes 131104 | tf_op jit(solution)/shard_map/ppermute | solution.py:293
  74.1 1.7 %weigh.3 = (f32[16,16,2048]{2,1,0:T(8,128)}, f32[1,16]{1,0:T(1,128)}) custom-call(s32[3]{0:T(128)S(1)} %pad_add_fusion.me_ref, bf16[8,16,512]{2,1,0:T(8,128)(2,1)S(1)} %get-tuple-element.59.refs_0_, bf16[8,16,512]{2,1,0:T(8,128)(2,1)S(1)} %collective-permute-done.14.refs_1_, ...), custom_call_target="tpu_custom_call", output_to_operand_aliasing={{0}: (5, {})} | custom-call | tf_op jit(solution)/shard_map/weigh/pallas_call | solution.py:263
  (9 shorter events, 0.2 us)
Async XLA Ops:
  0.6 16.4 %collective-permute-start.4 = (bf16[512,4096]{1,0:T(8,128)(2,1)}, bf16[512,4096]{1,0:T(8,128)(2,1)}, u32[]{:S(2)}, u32[]{:S(2)}) collective-permute-start(bf16[512,4096]{1,0:T(8,128)(2,1)} %bitcast.33), channel_id=1, source_target_pairs={{0,4},{4,0},{8,12},{12,8},{1,5},{5,1},{9,13},{13,9},{2,6},{6,2},{1... | collective-permute-start | bytes 12582920 | tf_op jit(solution)/shard_map/ppermute | solution.py:297
  2.8 7.9 %collective-permute-start.2 = (bf16[8,4224]{1,0:T(8,128)(2,1)}, bf16[8,4224]{1,0:T(8,128)(2,1)S(1)}, u32[]{:S(2)}, u32[]{:S(2)}) collective-permute-start(bf16[8,4224]{1,0:T(8,128)(2,1)} %get-tuple-element.29), channel_id=1, source_target_pairs={{0,3},{1,2},{2,1},{3,0},{4,7},{5,6},{6,5},{7,4},{8,11},{9,10},{10,... | collective-permute-start | bytes 202760 | tf_op jit(solution)/shard_map/ppermute | solution.py:293
  7.4 6.6 %collective-permute-start = (bf16[8,4224]{1,0:T(8,128)(2,1)}, bf16[8,4224]{1,0:T(8,128)(2,1)S(1)}, u32[]{:S(2)}, u32[]{:S(2)}) collective-permute-start(bf16[8,4224]{1,0:T(8,128)(2,1)} %get-tuple-element.29), channel_id=1, source_target_pairs={{0,1},{1,0},{2,3},{3,2},{4,5},{5,4},{6,7},{7,6},{8,9},{9,8},{10,11... | collective-permute-start | bytes 202760 | tf_op jit(solution)/shard_map/ppermute | solution.py:293
  7.4 7.0 %collective-permute-start.1 = (bf16[8,4224]{1,0:T(8,128)(2,1)}, bf16[8,4224]{1,0:T(8,128)(2,1)S(1)}, u32[]{:S(2)}, u32[]{:S(2)}) collective-permute-start(bf16[8,4224]{1,0:T(8,128)(2,1)} %get-tuple-element.29), channel_id=1, source_target_pairs={{0,2},{1,3},{2,0},{3,1},{4,6},{5,7},{6,4},{7,5},{8,10},{9,11},{10,... | collective-permute-start | bytes 202760 | tf_op jit(solution)/shard_map/ppermute | solution.py:293
  8.0 16.0 %collective-permute-start.5 = (bf16[8,4224]{1,0:T(8,128)(2,1)}, bf16[8,4224]{1,0:T(8,128)(2,1)S(1)}, u32[]{:S(2)}, u32[]{:S(2)}) collective-permute-start(bf16[8,4224]{1,0:T(8,128)(2,1)} %get-tuple-element.39), channel_id=1, source_target_pairs={{0,1},{1,0},{2,3},{3,2},{4,5},{5,4},{6,7},{7,6},{8,9},{9,8},{10,11... | collective-permute-start | bytes 202760 | tf_op jit(solution)/shard_map/ppermute | solution.py:293
  10.7 13.4 %collective-permute-start.6 = (bf16[8,4224]{1,0:T(8,128)(2,1)}, bf16[8,4224]{1,0:T(8,128)(2,1)S(1)}, u32[]{:S(2)}, u32[]{:S(2)}) collective-permute-start(bf16[8,4224]{1,0:T(8,128)(2,1)} %get-tuple-element.39), channel_id=1, source_target_pairs={{0,2},{1,3},{2,0},{3,1},{4,6},{5,7},{6,4},{7,5},{8,10},{9,11},{10,... | collective-permute-start | bytes 202760 | tf_op jit(solution)/shard_map/ppermute | solution.py:293
  14.1 10.0 %collective-permute-start.7 = (bf16[8,4224]{1,0:T(8,128)(2,1)}, bf16[8,4224]{1,0:T(8,128)(2,1)S(1)}, u32[]{:S(2)}, u32[]{:S(2)}) collective-permute-start(bf16[8,4224]{1,0:T(8,128)(2,1)} %get-tuple-element.39), channel_id=1, source_target_pairs={{0,3},{1,2},{2,1},{3,0},{4,7},{5,6},{6,5},{7,4},{8,11},{9,10},{10,... | collective-permute-start | bytes 202760 | tf_op jit(solution)/shard_map/ppermute | solution.py:293
  15.3 14.3 %collective-permute-start.3 = (bf16[4,8,4224]{2,1,0:T(8,128)(2,1)S(1)}, bf16[4,8,4224]{2,1,0:T(8,128)(2,1)S(1)}, u32[]{:S(2)}, u32[]{:S(2)}) collective-permute-start(bf16[4,8,4224]{2,1,0:T(8,128)(2,1)S(1)} %pad_maximum_fusion.rows_ref), channel_id=1, source_target_pairs={{0,8},{4,12},{8,0},{12,4},{1,9},{5,13},{9,1},{13,5},{2,10},{6,14},... | collective-permute-start | bytes 811016 | tf_op jit(solution)/shard_map/ppermute | solution.py:290
  17.1 2.2 %copy-start = (bf16[1,512,4096]{2,1,0:T(8,128)(2,1)S(1)}, bf16[1,512,4096]{2,1,0:T(8,128)(2,1)}, u32[]{:S(2)}) copy-start(bf16[1,512,4096]{2,1,0:T(8,128)(2,1)} %param.11) | copy-start | bytes 12582916
  19.2 4.8 %copy-start.1 = (bf16[8,4224]{1,0:T(8,128)(2,1)S(1)}, bf16[8,4224]{1,0:T(8,128)(2,1)}, u32[]{:S(2)}) copy-start(bf16[8,4224]{1,0:T(8,128)(2,1)} %get-tuple-element.39) | copy-start | bytes 202756
  24.1 11.7 %collective-permute-start.8 = (bf16[4,8,4224]{2,1,0:T(8,128)(2,1)S(1)}, bf16[4,8,4224]{2,1,0:T(8,128)(2,1)S(1)}, u32[]{:S(2)}, u32[]{:S(2)}) collective-permute-start(bf16[4,8,4224]{2,1,0:T(8,128)(2,1)S(1)} %pad_maximum_fusion.1.rows_ref), channel_id=1, source_target_pairs={{0,8},{4,12},{8,0},{12,4},{1,9},{5,13},{9,1},{13,5},{2,10},{6,14},... | collective-permute-start | bytes 811016 | tf_op jit(solution)/shard_map/ppermute | solution.py:290
  35.6 14.9 %collective-permute-start.10 = (bf16[4,8,16,512]{3,2,1,0:T(8,128)(2,1)S(1)}, bf16[4,8,16,512]{3,2,1,0:T(8,128)(2,1)S(1)}, u32[]{:S(2)}, u32[]{:S(2)}) collective-permute-start(bf16[4,8,16,512]{3,2,1,0:T(8,128)(2,1)S(1)} %score.6), channel_id=1, source_target_pairs={{0,8},{4,12},{8,0},{12,4},{1,9},{5,13},{9,1},{13,5},{2,10},{6,14},... | collective-permute-start | bytes 1572872 | tf_op jit(solution)/shard_map/ppermute | solution.py:290
  41.7 20.3 %collective-permute-start.9 = (bf16[4,8,16,512]{3,2,1,0:T(8,128)(2,1)S(1)}, bf16[4,8,16,512]{3,2,1,0:T(8,128)(2,1)S(1)}, u32[]{:S(2)}, u32[]{:S(2)}) collective-permute-start(bf16[4,8,16,512]{3,2,1,0:T(8,128)(2,1)S(1)} %score.5), channel_id=1, source_target_pairs={{0,8},{4,12},{8,0},{12,4},{1,9},{5,13},{9,1},{13,5},{2,10},{6,14},... | collective-permute-start | bytes 1572872 | tf_op jit(solution)/shard_map/ppermute | solution.py:290
  50.7 10.3 %collective-permute-start.11 = (bf16[8,16,512]{2,1,0:T(8,128)(2,1)S(1)}, bf16[8,16,512]{2,1,0:T(8,128)(2,1)S(1)}, u32[]{:S(2)}, u32[]{:S(2)}) collective-permute-start(bf16[8,16,512]{2,1,0:T(8,128)(2,1)S(1)} %get-tuple-element.62), channel_id=1, source_target_pairs={{0,1},{1,0},{2,3},{3,2},{4,5},{5,4},{6,7},{7,6},{8,9},{9,8},{10,11... | collective-permute-start | bytes 393224 | tf_op jit(solution)/shard_map/ppermute | solution.py:293
  51.7 9.3 %collective-permute-start.12 = (bf16[8,16,512]{2,1,0:T(8,128)(2,1)S(1)}, bf16[8,16,512]{2,1,0:T(8,128)(2,1)S(1)}, u32[]{:S(2)}, u32[]{:S(2)}) collective-permute-start(bf16[8,16,512]{2,1,0:T(8,128)(2,1)S(1)} %get-tuple-element.61), channel_id=1, source_target_pairs={{0,2},{1,3},{2,0},{3,1},{4,6},{5,7},{6,4},{7,5},{8,10},{9,11},{10,... | collective-permute-start | bytes 393224 | tf_op jit(solution)/shard_map/ppermute | solution.py:293
  54.9 7.1 %collective-permute-start.13 = (bf16[8,16,512]{2,1,0:T(8,128)(2,1)S(1)}, bf16[8,16,512]{2,1,0:T(8,128)(2,1)S(1)}, u32[]{:S(2)}, u32[]{:S(2)}) collective-permute-start(bf16[8,16,512]{2,1,0:T(8,128)(2,1)S(1)} %get-tuple-element.60), channel_id=1, source_target_pairs={{0,3},{1,2},{2,1},{3,0},{4,7},{5,6},{6,5},{7,4},{8,11},{9,10},{10,... | collective-permute-start | bytes 393224 | tf_op jit(solution)/shard_map/ppermute | solution.py:293
  62.2 7.8 %collective-permute-start.14 = (bf16[8,16,512]{2,1,0:T(8,128)(2,1)S(1)}, bf16[8,16,512]{2,1,0:T(8,128)(2,1)S(1)}, u32[]{:S(2)}, u32[]{:S(2)}) collective-permute-start(bf16[8,16,512]{2,1,0:T(8,128)(2,1)S(1)} %get-tuple-element.58), channel_id=1, source_target_pairs={{0,1},{1,0},{2,3},{3,2},{4,5},{5,4},{6,7},{7,6},{8,9},{9,8},{10,11... | collective-permute-start | bytes 393224 | tf_op jit(solution)/shard_map/ppermute | solution.py:293
  63.1 6.9 %collective-permute-start.15 = (bf16[8,16,512]{2,1,0:T(8,128)(2,1)S(1)}, bf16[8,16,512]{2,1,0:T(8,128)(2,1)S(1)}, u32[]{:S(2)}, u32[]{:S(2)}) collective-permute-start(bf16[8,16,512]{2,1,0:T(8,128)(2,1)S(1)} %get-tuple-element.57), channel_id=1, source_target_pairs={{0,2},{1,3},{2,0},{3,1},{4,6},{5,7},{6,4},{7,5},{8,10},{9,11},{10,... | collective-permute-start | bytes 393224 | tf_op jit(solution)/shard_map/ppermute | solution.py:293
  66.8 7.2 %collective-permute-start.16 = (bf16[8,16,512]{2,1,0:T(8,128)(2,1)S(1)}, bf16[8,16,512]{2,1,0:T(8,128)(2,1)S(1)}, u32[]{:S(2)}, u32[]{:S(2)}) collective-permute-start(bf16[8,16,512]{2,1,0:T(8,128)(2,1)S(1)} %get-tuple-element.56), channel_id=1, source_target_pairs={{0,3},{1,2},{2,1},{3,0},{4,7},{5,6},{6,5},{7,4},{8,11},{9,10},{10,... | collective-permute-start | bytes 393224 | tf_op jit(solution)/shard_map/ppermute | solution.py:293
